TPU v7x, 32 devices: a whole 2x2x4 slice. The times are simulated.
32 devices in a mesh: rep: 4 (over z), exp: 8 (over y, x, core).
Axes of the slice: x: 2, y: 2, z: 4, core: 2. Of those that a mesh axis runs over, the one named last changes fastest.
Arguments:
- tokens: bfloat16 [36864, 768], P(('rep', 'exp')), may hold values from -6 to 6
- cotangent: bfloat16 [36864, 768], P(('rep', 'exp')), may hold values from -6 to 6
- expert_ids: int32 [36864, 2], P(('rep', 'exp')), may hold values from 0 to 7, as said below
- expert_slots: int32 [36864, 2], P(('rep', 'exp')), may hold values from -1 to 143, as said below
- w_qkv: bfloat16 [768, 2304], replicated, may hold values from -0.21875 to 0.21875
- q_bias: bfloat16 [768], replicated, may hold values from -1.75 to 1.75
- v_bias: bfloat16 [768], replicated, may hold values from -1.75 to 1.75
- w_proj: bfloat16 [768, 768], replicated, may hold values from -0.875 to 0.875
- proj_bias: bfloat16 [768], replicated, may hold values from -1.75 to 1.75
- gain_one: float32 [768], replicated, may hold values from 0.25 to 1.75
- shift_one: float32 [768], replicated, may hold values from -1.75 to 1.75
- gain_two: float32 [768], replicated, may hold values from 0.25 to 1.75
- shift_two: float32 [768], replicated, may hold values from -1.75 to 1.75
- w_router: float32 [768, 8], replicated, may hold values from -0.15625 to 0.15625
- expert_in: bfloat16 [8, 768, 3072], P('exp'), may hold values from -0.21875 to 0.21875
- expert_in_bias: bfloat16 [8, 3072], P('exp'), may hold values from -1.75 to 1.75
- expert_out: bfloat16 [8, 3072, 768], P('exp'), may hold values from -0.4375 to 0.4375
- expert_out_bias: bfloat16 [8, 768], P('exp'), may hold values from -1.5 to 1.5
Outputs:
- mixed: bfloat16 [36864, 768], P(('rep', 'exp'))
- grad_tokens: float32 [36864, 768], P(('rep', 'exp'))
- grad_w_qkv: float32 [768, 2304], replicated
- grad_q_bias: float32 [768], replicated
- grad_v_bias: float32 [768], replicated
- grad_w_proj: float32 [768, 768], replicated
- grad_proj_bias: float32 [768], replicated
- grad_gain_one: float32 [768], replicated
- grad_shift_one: float32 [768], replicated
- grad_gain_two: float32 [768], replicated
- grad_shift_two: float32 [768], replicated
- grad_w_router: float32 [768, 8], replicated
- grad_expert_in: float32 [8, 768, 3072], P('exp', None, 'rep')
- grad_expert_in_bias: float32 [8, 3072], P('exp', 'rep')
- grad_expert_out: float32 [8, 3072, 768], P('exp', 'rep')
- grad_expert_out_bias: float32 [8, 768], P('exp', 'rep')
Inputs may be any that keep to these rules, and one draw needn't show every extreme that they name: `expert_ids`: the two experts of a patch differ. `expert_slots`: among the pairs of one device (aligned blocks of 1152 rows), each expert's kept pairs hold the slots 0, 1, 2, ... once each in a priority order of those pairs, and a pair is -1 exactly when its expert already has 144 pairs of that device before it.
All inputs are finite; a program needn't handle non-finite values.
Results may differ from a plain program's by a relative error of at most 0.014.
Values may be sent and summed in bfloat16 or wider, within the bound.
No kernel may reach another device: no remote copies, remote signals or barrier semaphores. Data moves between devices by JAX's collectives and lax.ppermute only.
A program may use at most 192 MiB of HBM per device.

v0:
```python
import jax
import jax.numpy as jnp
from jax import lax
from jax.sharding import PartitionSpec as P

HEADS = 12
HEAD_DIM = 64
SEQ = 576
EPSILON = 1e-06
HIGHEST = lax.Precision.HIGHEST


def norm_forward(field, norm_gain, norm_shift):
    average = jnp.mean(field, axis=-1, keepdims=True)
    centred = field - average
    variance = jnp.mean(centred * centred, axis=-1, keepdims=True)
    inverse = lax.rsqrt(variance + EPSILON)
    unit_rows = centred * inverse
    return (unit_rows * norm_gain + norm_shift, unit_rows, inverse)


def norm_backward(grad_out, unit_rows, inverse, norm_gain):
    grad_unit = grad_out * norm_gain
    centred = grad_unit - jnp.mean(grad_unit, axis=-1, keepdims=True)
    along = unit_rows * jnp.mean(grad_unit * unit_rows, axis=-1, keepdims=True)
    return (
        inverse * (centred - along),
        jnp.sum(grad_out * unit_rows, axis=0),
        jnp.sum(grad_out, axis=0),
    )


def by_heads(block):
    return block.reshape(block.shape[0], HEADS, HEAD_DIM)


def contract_last(left, right):
    return lax.dot_general(
        left, right, (((1,), (1,)), ((), ())), preferred_element_type=jnp.float32
    )


def contract_first(left, right):
    return lax.dot_general(
        left, right, (((0,), (0,)), ((), ())), preferred_element_type=jnp.float32
    )


def contract_first_high(left, right):
    return lax.dot_general(
        left, right, (((0,), (0,)), ((), ())), precision=HIGHEST, preferred_element_type=jnp.float32
    )


def exact_gelu(field):
    return jax.nn.gelu(field, approximate=False)


def image_scores(queries, key_rows):
    return jnp.einsum(
        "qhd,khd->hqk", by_heads(queries), by_heads(key_rows), preferred_element_type=jnp.float32
    ) * HEAD_DIM ** (-0.5)


def attend_image(pieces):
    queries, key_rows, values = pieces
    scores = image_scores(queries, key_rows)
    row_max = jnp.max(scores, axis=-1, keepdims=True)
    exponent = jnp.exp(scores - row_max)
    row_total = jnp.sum(exponent, axis=-1, keepdims=True)
    weights = (exponent / row_total).astype(jnp.bfloat16)
    context = jnp.einsum(
        "hqk,khd->qhd", weights, by_heads(values), preferred_element_type=jnp.float32
    )
    return (context.reshape(queries.shape[0], -1), (row_max + jnp.log(row_total))[..., 0])


def attend_back(pieces):
    queries, key_rows, values, grad_context, log_total = pieces
    scores = image_scores(queries, key_rows)
    probs = jnp.exp(scores - log_total[..., None])
    weights = probs.astype(jnp.bfloat16)
    grad_heads = by_heads(grad_context)
    grad_probs = jnp.einsum(
        "qhd,khd->hqk", grad_heads, by_heads(values), preferred_element_type=jnp.float32
    )
    grad_values = jnp.einsum(
        "hqk,qhd->khd", weights, grad_heads, preferred_element_type=jnp.float32
    )
    grad_scores = (
        probs * (grad_probs - jnp.sum(probs * grad_probs, axis=-1, keepdims=True))
    ).astype(jnp.bfloat16)
    grad_queries = jnp.einsum(
        "hqk,khd->qhd", grad_scores, by_heads(key_rows), preferred_element_type=jnp.float32
    ) * HEAD_DIM ** (-0.5)
    grad_keys = jnp.einsum(
        "hqk,qhd->khd", grad_scores, by_heads(queries), preferred_element_type=jnp.float32
    ) * HEAD_DIM ** (-0.5)
    length = queries.shape[0]
    joined = jnp.concatenate(
        [
            grad_queries.reshape(length, -1),
            grad_keys.reshape(length, -1),
            grad_values.reshape(length, -1),
        ],
        axis=1,
    )
    return joined.astype(jnp.bfloat16)


def expert_backward(rows_in, grads_out, weight_in, bias_in, weight_out):
    hidden = jnp.dot(rows_in, weight_in, preferred_element_type=jnp.float32) + bias_in
    activated, gelu_back = jax.vjp(exact_gelu, hidden)
    grad_hidden = gelu_back(contract_last(grads_out, weight_out))[0].astype(jnp.bfloat16)
    return (activated.astype(jnp.bfloat16), grad_hidden)


def on_device(
    tokens,
    cotangent,
    expert_ids,
    expert_slots,
    w_qkv,
    q_bias,
    v_bias,
    w_proj,
    proj_bias,
    gain_one,
    shift_one,
    gain_two,
    shift_two,
    w_router,
    expert_in,
    expert_in_bias,
    expert_out,
    expert_out_bias,
):
    row_count, model_width = tokens.shape
    experts = w_router.shape[1]
    slot_count = row_count // experts
    images = row_count // SEQ
    inputs = tokens.astype(jnp.float32)
    normed_one, unit_one, inverse_one = norm_forward(inputs, gain_one, shift_one)
    normed_one = normed_one.astype(jnp.bfloat16)
    bias_row = jnp.concatenate(
        [
            q_bias.astype(jnp.float32),
            jnp.zeros((model_width,), jnp.float32),
            v_bias.astype(jnp.float32),
        ]
    )
    projected = (jnp.dot(normed_one, w_qkv, preferred_element_type=jnp.float32) + bias_row).astype(
        jnp.bfloat16
    )
    image_blocks = projected.reshape(images, SEQ, 3 * model_width)
    query_blocks = image_blocks[:, :, :model_width]
    key_blocks = image_blocks[:, :, model_width : 2 * model_width]
    value_blocks = image_blocks[:, :, 2 * model_width :]
    context, log_total = lax.map(attend_image, (query_blocks, key_blocks, value_blocks))
    context = context.reshape(row_count, model_width).astype(jnp.bfloat16)
    branch = jnp.dot(context, w_proj, preferred_element_type=jnp.float32) + proj_bias.astype(
        jnp.float32
    )
    residual = inputs + branch
    normed_two, unit_two, inverse_two = norm_forward(residual, gain_two, shift_two)
    normed_two = normed_two.astype(jnp.bfloat16)
    router = jax.nn.softmax(
        jnp.dot(normed_two.astype(jnp.float32), w_router, precision=HIGHEST), axis=-1
    )
    columns = jnp.where(expert_slots >= 0, expert_ids * slot_count + expert_slots, -1)
    target = lax.broadcasted_iota(jnp.int32, (1, experts * slot_count), 1)
    first_hit = (columns[:, 0:1] == target).astype(jnp.bfloat16)
    second_hit = (columns[:, 1:2] == target).astype(jnp.bfloat16)
    either = first_hit + second_hit
    hits = jnp.concatenate([first_hit, second_hit], axis=0)
    chosen = (expert_ids[:, :, None] == lax.broadcasted_iota(jnp.int32, (1, 1, experts), 2)).astype(
        jnp.float32
    )
    gate_values = jnp.sum(router[:, None, :] * chosen, axis=-1)
    outgoing = (
        contract_first(either, normed_two)
        .astype(jnp.bfloat16)
        .reshape(experts, slot_count, model_width)
    )
    arrived = lax.all_to_all(outgoing, "exp", split_axis=0, concat_axis=0, tiled=True).reshape(
        row_count, model_width
    )
    weight_in = expert_in[0]
    bias_in = expert_in_bias[0].astype(jnp.float32)
    weight_out = expert_out[0]
    bias_out = expert_out_bias[0].astype(jnp.float32)
    hidden = jnp.dot(arrived, weight_in, preferred_element_type=jnp.float32) + bias_in
    activated = exact_gelu(hidden).astype(jnp.bfloat16)
    produced = (
        jnp.dot(activated, weight_out, preferred_element_type=jnp.float32) + bias_out
    ).astype(jnp.bfloat16)
    returned = lax.all_to_all(
        produced.reshape(experts, slot_count, model_width),
        "exp",
        split_axis=0,
        concat_axis=0,
        tiled=True,
    ).reshape(row_count, model_width)
    picked_both = jnp.dot(hits, returned, preferred_element_type=jnp.float32)
    picked_first = picked_both[:row_count]
    picked_second = picked_both[row_count:]
    final = residual + gate_values[:, 0:1] * picked_first + gate_values[:, 1:2] * picked_second
    mixed = final.astype(jnp.bfloat16)
    grad_out = cotangent.astype(jnp.float32)
    grad_gates = jnp.stack(
        [jnp.sum(grad_out * picked_first, axis=-1), jnp.sum(grad_out * picked_second, axis=-1)],
        axis=-1,
    )
    grad_router = jnp.sum(grad_gates[:, :, None] * chosen, axis=1)
    grad_logits = router * (grad_router - jnp.sum(router * grad_router, axis=-1, keepdims=True))
    grad_picked = jnp.concatenate(
        [gate_values[:, 0:1] * grad_out, gate_values[:, 1:2] * grad_out], axis=0
    ).astype(jnp.bfloat16)
    grad_returned = (
        contract_first(hits, grad_picked)
        .astype(jnp.bfloat16)
        .reshape(experts, slot_count, model_width)
    )
    grad_produced = lax.all_to_all(
        grad_returned, "exp", split_axis=0, concat_axis=0, tiled=True
    ).reshape(row_count, model_width)
    act_round, grad_hidden = expert_backward(arrived, grad_produced, weight_in, bias_in, weight_out)
    grad_arrived = (
        contract_last(grad_hidden, weight_in)
        .astype(jnp.bfloat16)
        .reshape(experts, slot_count, model_width)
    )
    grad_source = lax.all_to_all(
        grad_arrived, "exp", split_axis=0, concat_axis=0, tiled=True
    ).reshape(row_count, model_width)
    local_in = contract_first(arrived, grad_hidden)[None]
    local_in_bias = jnp.sum(grad_hidden.astype(jnp.float32), axis=0)[None]
    local_out = contract_first(act_round, grad_produced)[None]
    local_out_bias = jnp.sum(grad_produced.astype(jnp.float32), axis=0)[None]
    grad_ein, grad_einb, grad_eout, grad_eoutb = (
        lax.psum_scatter(
            local_in.astype(jnp.bfloat16), "rep", scatter_dimension=2, tiled=True
        ).astype(jnp.float32),
        lax.psum_scatter(
            local_in_bias.astype(jnp.bfloat16), "rep", scatter_dimension=1, tiled=True
        ).astype(jnp.float32),
        lax.psum_scatter(
            local_out.astype(jnp.bfloat16), "rep", scatter_dimension=1, tiled=True
        ).astype(jnp.float32),
        lax.psum_scatter(
            local_out_bias.astype(jnp.bfloat16), "rep", scatter_dimension=1, tiled=True
        ).astype(jnp.float32),
    )
    grad_normed_two = jnp.dot(either, grad_source, preferred_element_type=jnp.float32)
    grad_normed_two = grad_normed_two + lax.dot_general(
        grad_logits,
        w_router,
        (((1,), (1,)), ((), ())),
        precision=HIGHEST,
        preferred_element_type=jnp.float32,
    )
    local_router = contract_first_high(normed_two.astype(jnp.float32), grad_logits)
    grad_from_norm, local_gain_two, local_shift_two = norm_backward(
        grad_normed_two, unit_two, inverse_two, gain_two
    )
    grad_residual = grad_out + grad_from_norm
    grad_branch = grad_residual.astype(jnp.bfloat16)
    local_proj = contract_first(context, grad_branch)
    local_proj_bias = jnp.sum(grad_branch.astype(jnp.float32), axis=0)
    grad_context = contract_last(grad_branch, w_proj).astype(jnp.bfloat16)
    grad_qkv = lax.map(
        attend_back,
        (
            query_blocks,
            key_blocks,
            value_blocks,
            grad_context.reshape(images, SEQ, model_width),
            log_total,
        ),
    )
    grad_qkv = grad_qkv.reshape(row_count, 3 * model_width)
    local_qkv = contract_first(normed_one, grad_qkv)
    grad_wide = grad_qkv.astype(jnp.float32)
    local_q_bias = jnp.sum(grad_wide[:, :model_width], axis=0)
    local_v_bias = jnp.sum(grad_wide[:, 2 * model_width :], axis=0)
    grad_normed_one = contract_last(grad_qkv, w_qkv)
    grad_from_first, local_gain_one, local_shift_one = norm_backward(
        grad_normed_one, unit_one, inverse_one, gain_one
    )
    grad_tokens = grad_residual + grad_from_first
    (
        grad_w_qkv,
        grad_q_bias,
        grad_v_bias,
        grad_w_proj,
        grad_proj_bias,
        grad_gain_one,
        grad_shift_one,
        grad_gain_two,
        grad_shift_two,
        grad_w_router,
    ) = lax.psum(
        (
            local_qkv,
            local_q_bias,
            local_v_bias,
            local_proj,
            local_proj_bias,
            local_gain_one,
            local_shift_one,
            local_gain_two,
            local_shift_two,
            local_router,
        ),
        ("rep", "exp"),
    )
    return (
        mixed,
        grad_tokens,
        grad_w_qkv,
        grad_q_bias,
        grad_v_bias,
        grad_w_proj,
        grad_proj_bias,
        grad_gain_one,
        grad_shift_one,
        grad_gain_two,
        grad_shift_two,
        grad_w_router,
        grad_ein,
        grad_einb,
        grad_eout,
        grad_eoutb,
    )


def solution(mesh):
    placed = (
        P(("rep", "exp"), None),
        P(("rep", "exp"), None),
        P(("rep", "exp"), None),
        P(("rep", "exp"), None),
        P(),
        P(),
        P(),
        P(),
        P(),
        P(),
        P(),
        P(),
        P(),
        P(),
        P("exp", None, None),
        P("exp", None),
        P("exp", None, None),
        P("exp", None),
    )
    return jax.shard_map(
        on_device,
        mesh=mesh,
        in_specs=placed,
        out_specs=(
            P(("rep", "exp"), None),
            P(("rep", "exp"), None),
            P(),
            P(),
            P(),
            P(),
            P(),
            P(),
            P(),
            P(),
            P(),
            P(),
            P("exp", None, "rep"),
            P("exp", "rep"),
            P("exp", "rep", None),
            P("exp", "rep"),
        ),
        check_vma=False,
    )
```

profile of v0, /device:TPU:0, one launch (start us, length us, event | category | flops | bytes accessed | tf_op | source)
XLA Modules:
  0.0 720.9 jit_solution(12045565676149617166)
XLA Ops:
  40.2 76.1 %while.22 = (s32[]{:T(128)}, bf16[2,576,768]{2,1,0:T(8,128)(2,1)}, f32[2,12,576]{2,1,0:T(8,128)}, bf16[2,576,768]{1,2,0:T(8,128)(2,1)}, bf16[2,576,768]{1,2,0:T(...) while((s32[]{:T(128)}, bf16[2,576,768]{2,1,0:T(8,128)(2,1)}, f32[2,12,576]{2,1,0:T(8,128)}, ...), condition=%wide.region_5.6_spmd, body=%wide.region_2.5_spmd.sunk | while | flops 1055040768 | bytes 61086932 | solution.py:159
  52.4 9.7 %fusion.143 = f32[12,576]{1,0:T(8,128)} fusion(f32[12,576,576]{1,2,0:T(8,128)} %get-tuple-element.347, f32[12,576]{1,0:T(8,128)} %get-tuple-element.348), kind=kLoop, calls=%fused_computation.3.clone.1 | loop fusion | flops 11937024 | bytes 15980544 | tf_op jit(solution)/shard_map/while/body/eval_jaxpr/reduce_sum | solution.py:70
  62.1 11.1 %fusion.144 = bf16[12,64,576]{2,1,0:T(8,128)(2,1)} fusion(bf16[576,12,64]{0,2,1:T(8,128)(2,1)} %bitcast.167, f32[12,576,576]{1,2,0:T(8,128)} %get-tuple-element.347, f32[12,576]{1,0:T(8,128)} %fusion.143, f32[12,576]{1,0:T(8,128)} %get-tuple-element.348), kind=kOutput, calls=%fused_computation.4.clone.1 | convolution fusion | flops 525533184 | bytes 17750016 | tf_op jit(solution)/shard_map/while/body/eval_jaxpr/hqk,khd->qhd/dot_general | solution.py:72
  90.1 9.7 %fusion.143 = f32[12,576]{1,0:T(8,128)} fusion(f32[12,576,576]{1,2,0:T(8,128)} %get-tuple-element.347, f32[12,576]{1,0:T(8,128)} %get-tuple-element.348), kind=kLoop, calls=%fused_computation.3.clone.1 | loop fusion | flops 11937024 | bytes 15980544 | tf_op jit(solution)/shard_map/while/body/eval_jaxpr/reduce_sum | solution.py:70
  99.8 11.1 %fusion.144 = bf16[12,64,576]{2,1,0:T(8,128)(2,1)} fusion(bf16[576,12,64]{0,2,1:T(8,128)(2,1)} %bitcast.167, f32[12,576,576]{1,2,0:T(8,128)} %get-tuple-element.347, f32[12,576]{1,0:T(8,128)} %fusion.143, f32[12,576]{1,0:T(8,128)} %get-tuple-element.348), kind=kOutput, calls=%fused_computation.4.clone.1 | convolution fusion | flops 525533184 | bytes 17750016 | tf_op jit(solution)/shard_map/while/body/eval_jaxpr/hqk,khd->qhd/dot_general | solution.py:72
  141.2 14.5 %all-to-all-done = bf16[8,144,768]{2,1,0:T(8,128)(2,1)} async-done(((bf16[8,144,768]{2,1,0:T(8,128)(2,1)}), bf16[8,144,768]{2,1,0:T(8,128)(2,1)}, u32[]{:S(2)}, u32[]{:S(2)}) %all-to-all-start) | async-done | bytes 1769504 | tf_op jit(solution)/shard_map/all_to_all | solution.py:185
  155.7 40.7 %multiply_convert_fusion.3 = (bf16[1152,3072]{1,0:T(8,128)(2,1)S(1)}, f32[1152,3072]{1,0:T(8,128)}, f32[1152,3072]{1,0:T(8,128)}) fusion(f32[3072]{0:T(1024)S(1)} %bitcast.180, bf16[1152,768]{1,0:T(8,128)(2,1)} %bitcast.20, bf16[1,768,3072]{2,1,0:T(8,128)(2,1)} %param.36), kind=kOutput, calls=%fused_computation.32 | convolution fusion | flops 5669388288 | bytes 41889792 | tf_op jit(solution)/shard_map/dot_general | solution.py:192
  213.1 17.7 %all-to-all-done.1 = bf16[8,144,768]{2,1,0:T(8,128)(2,1)} async-done(((bf16[8,144,768]{2,1,0:T(8,128)(2,1)}), bf16[8,144,768]{2,1,0:T(8,128)(2,1)}, u32[]{:S(2)}, u32[]{:S(2)}) %all-to-all-start.1) | async-done | bytes 1769504 | tf_op jit(solution)/shard_map/all_to_all | solution.py:197
  248.6 26.2 %all_to_all.20 = bf16[8,144,768]{2,1,0:T(8,128)(2,1)} all-to-all(bf16[8,144,768]{2,1,0:T(8,128)(2,1)S(1)} %bitcast.177), channel_id=1, replica_groups=mesh['rep'=4,'exp'=8] {'exp'}, dimensions={0} | all-to-all | bytes 3538944 | tf_op jit(solution)/shard_map/all_to_all | solution.py:224
  278.8 20.9 %fusion.86 = (bf16[3072]{0:T(1024)(128)(2,1)}, bf16[1152,3072]{1,0:T(8,128)(2,1)}) fusion(f32[1152,3072]{1,0:T(8,128)} %get-tuple-element.237, f32[1152,3072]{1,0:T(8,128)} %get-tuple-element.254, bf16[1152,768]{1,0:T(8,128)(2,1)} %bitcast.169, bf16[1,3072,768]{2,1,0:T(8,128)(2,1)} %param.38), kind=kOutput, calls=%fused_computation.154 | convolution fusion | flops 5488899072 | bytes 41883648 | tf_op jit(solution)/shard_map/dot_general | solution.py:38
  301.8 10.6 %fusion.28 = bf16[1,3072,768]{2,1,0:T(8,128)(2,1)} fusion(bf16[1152,3072]{1,0:T(8,128)(2,1)} %copy-done.59, bf16[1152,768]{1,0:T(8,128)(2,1)} %bitcast.170), kind=kOutput, calls=%fused_computation.71 | convolution fusion | flops 5438177280 | bytes 13565952 | tf_op jit(solution)/shard_map/dot_general | solution.py:44
  313.9 10.3 %fusion.55 = bf16[1152,768]{1,0:T(8,128)(2,1)} fusion(bf16[1152,3072]{1,0:T(8,128)(2,1)} %get-tuple-element.261, bf16[1,768,3072]{2,1,0:T(8,128)(2,1)} %param.36), kind=kOutput, calls=%fused_computation.106 | convolution fusion | flops 5436702720 | bytes 13565952 | tf_op jit(solution)/shard_map/dot_general | solution.py:38
  332.3 11.2 %fusion.27 = bf16[1,768,3072]{2,1,0:T(8,128)(2,1)} fusion(bf16[1152,768]{1,0:T(8,128)(2,1)} %bitcast.20, bf16[1152,3072]{1,0:T(8,128)(2,1)} %get-tuple-element.261), kind=kOutput, calls=%fused_computation.70 | convolution fusion | flops 5438177280 | bytes 13565952 | tf_op jit(solution)/shard_map/dot_general | solution.py:44
  372.1 131.4 %while.23 = (s32[]{:T(128)}, bf16[2,576,2304]{2,1,0:T(8,128)(2,1)}, bf16[2,576,768]{1,2,0:T(8,128)(2,1)}, bf16[2,576,768]{1,2,0:T(8,128)(2,1)}, f32[2,12,576]{2,...) while((s32[]{:T(128)}, bf16[2,576,2304]{2,1,0:T(8,128)(2,1)}, ...), condition=%wide.region_19.20_spmd, body=%wide.region_17.19_spmd.sunk | while | flops 2605982976 | bytes 160441552 | solution.py:271
  388.7 10.2 %fusion.156 = bf16[12,64,576]{2,1,0:T(8,128)(2,1)} fusion(bf16[576,12,64]{0,2,1:T(8,128)(2,1)S(1)} %bitcast.154, f32[12,576,576]{1,2,0:T(8,128)} %fusion.155, f32[12,576]{1,0:T(8,128)S(1)} %copy-done.11), kind=kOutput, calls=%fused_computation.21.clone.1 | convolution fusion | flops 521994240 | bytes 17722368 | tf_op jit(solution)/shard_map/while/body/eval_jaxpr/hqk,qhd->khd/dot_general | solution.py:87
  398.9 11.7 %multiply_reduce_fusion.11 = (f32[12,576]{1,0:T(8,128)S(1)}, f32[12,576,576]{1,2,0:T(8,128)}) fusion(f32[12,576,576]{1,2,0:T(8,128)} %fusion.155, f32[12,576]{1,0:T(8,128)S(1)} %copy-done.11, bf16[576,12,64]{0,2,1:T(8,128)(2,1)S(1)} %bitcast.155, bf16[576,12,64]{0,2,1:T(8,128)(2,1)S(1)} %bitcast.160), kind=kOutput, calls=%fused_computation.12.clone.1 | convolution fusion | flops 525526272 | bytes 33675264 | tf_op jit(solution)/shard_map/while/body/eval_jaxpr/qhd,khd->hqk/dot_general | solution.py:84
  410.6 13.3 %multiply_convert_fusion.7 = bf16[12,576,576]{1,2,0:T(8,128)(2,1)S(1)} fusion(f32[12,576,576]{1,2,0:T(8,128)} %get-tuple-element.358, f32[12,576,576]{1,2,0:T(8,128)} %fusion.155, f32[12,576]{1,0:T(8,128)S(1)} %get-tuple-element.359, f32[12,576]{1,0:T(8,128)S(1)} %copy-done.11), kind=kLoop, calls=%fused_computation.11.clone.1 | loop fusion | flops 19906560 | bytes 39868416 | tf_op jit(solution)/shard_map/while/body/eval_jaxpr/convert_element_type | solution.py:92
  454.6 10.2 %fusion.156 = bf16[12,64,576]{2,1,0:T(8,128)(2,1)} fusion(bf16[576,12,64]{0,2,1:T(8,128)(2,1)S(1)} %bitcast.154, f32[12,576,576]{1,2,0:T(8,128)} %fusion.155, f32[12,576]{1,0:T(8,128)S(1)} %copy-done.11), kind=kOutput, calls=%fused_computation.21.clone.1 | convolution fusion | flops 521994240 | bytes 17722368 | tf_op jit(solution)/shard_map/while/body/eval_jaxpr/hqk,qhd->khd/dot_general | solution.py:87
  464.8 11.7 %multiply_reduce_fusion.11 = (f32[12,576]{1,0:T(8,128)S(1)}, f32[12,576,576]{1,2,0:T(8,128)}) fusion(f32[12,576,576]{1,2,0:T(8,128)} %fusion.155, f32[12,576]{1,0:T(8,128)S(1)} %copy-done.11, bf16[576,12,64]{0,2,1:T(8,128)(2,1)S(1)} %bitcast.155, bf16[576,12,64]{0,2,1:T(8,128)(2,1)S(1)} %bitcast.160), kind=kOutput, calls=%fused_computation.12.clone.1 | convolution fusion | flops 525526272 | bytes 33675264 | tf_op jit(solution)/shard_map/while/body/eval_jaxpr/qhd,khd->hqk/dot_general | solution.py:84
  476.6 12.5 %multiply_convert_fusion.7 = bf16[12,576,576]{1,2,0:T(8,128)(2,1)S(1)} fusion(f32[12,576,576]{1,2,0:T(8,128)} %get-tuple-element.358, f32[12,576,576]{1,2,0:T(8,128)} %fusion.155, f32[12,576]{1,0:T(8,128)S(1)} %get-tuple-element.359, f32[12,576]{1,0:T(8,128)S(1)} %copy-done.11), kind=kLoop, calls=%fused_computation.11.clone.1 | loop fusion | flops 19906560 | bytes 39868416 | tf_op jit(solution)/shard_map/while/body/eval_jaxpr/convert_element_type | solution.py:92
  503.5 11.1 %fusion.78 = f32[768,2304]{1,0:T(8,128)} fusion(bf16[1152,2304]{1,0:T(8,128)(2,1)} %bitcast.172, bf16[1152,768]{0,1:T(8,128)(2,1)} %copy.98, f32[768]{0:T(1024)} %param.32, f32[768]{0:T(1024)} %param.31, f32[1152]{0:T(1024)S(1)} %copy-done.39, f32[1152]{0:T(1024)S(1)} %copy-done.32), kind=kOutput, calls=%fused_computation.149 | convolution fusion | flops 4082171904 | bytes 14171136 | tf_op jit(solution)/shard_map/dot_general | solution.py:44
  514.6 9.2 %fusion.85 = (f32[768]{0:T(1024)}, f32[1152,768]{1,0:T(8,128)}) fusion(bf16[1152,2304]{1,0:T(8,128)(2,1)} %bitcast.173, bf16[768,2304]{1,0:T(8,128)(2,1)S(1)} %copy-done), kind=kOutput, calls=%fused_computation.153 | convolution fusion | flops 4077747456 | bytes 12389376 | tf_op jit(solution)/shard_map/dot_general | solution.py:38
  551.8 41.6 %all-reduce = (f32[768]{0:T(1024)}, f32[768]{0:T(1024)}, f32[768]{0:T(1024)}, f32[768]{0:T(1024)}, f32[768]{0:T(1024)}, /*index=5*/f32[768]{0:T(1024)}, f32[768]{0:T(1024)}, f32[768,8]{0,1:T(8,128)}) all-reduce(f32[768]{0:T(1024)S(1)} %get-tuple-element.182, ...), channel_id=1, replica_groups=mesh['rep'=4,'exp'=8] {'rep','exp'}, use_global_device_ids=true, to_apply=%region_24.25 | all-reduce | flops 11520 | bytes 92160 | tf_op jit(solution)/shard_map/psum | solution.py:302
  599.2 106.4 %all-reduce.4.cloned.1.call-done = (f32[768,2304]{1,0:T(8,128)}, f32[768,768]{1,0:T(8,128)}) async-done(((f32[768,2304]{1,0:T(8,128)}, f32[768,768]{1,0:T(8,128)}), (f32[768,2304]{1,0:T(8,128)}, f32[768,768]{1,0:T(8,128)})) %all-reduce.4.cloned.1.call-update) | async-done | bytes 9437200 | tf_op jit(solution)/shard_map/psum | solution.py:302
  (263 shorter events, 271.6 us)
Async XLA Ops:
  8.0 12.2 %copy-start = (bf16[768,2304]{1,0:T(8,128)(2,1)S(1)}, bf16[768,2304]{1,0:T(8,128)(2,1)}, u32[]{:S(2)}) copy-start(bf16[768,2304]{1,0:T(8,128)(2,1)} %param.26) | copy-start | bytes 10616836
  40.2 76.2 %copy-start.52 = (f32[768]{0:T(1024)S(1)}, f32[768]{0:T(1024)}, u32[]{:S(2)}) copy-start(f32[768]{0:T(1024)} %convert_element_type.153) | copy-start | bytes 9220
  62.1 11.1 %copy-start.14 = (f32[12,576]{1,0:T(8,128)S(1)}, f32[12,576]{1,0:T(8,128)}, u32[]{:S(2)}) copy-start(f32[12,576]{1,0:T(8,128)} %get-tuple-element.348) | copy-start | bytes 82948 | tf_op jit(solution)/shard_map/while
  62.1 11.1 %copy-start.15 = (f32[12,576]{1,0:T(8,128)S(1)}, f32[12,576]{1,0:T(8,128)}, u32[]{:S(2)}) copy-start(f32[12,576]{1,0:T(8,128)} %fusion.143) | copy-start | bytes 82948 | tf_op jit(solution)/shard_map/while
  62.1 11.1 %copy-start.23 = (f32[2,12,576]{2,1,0:T(8,128)S(1)}, f32[2,12,576]{2,1,0:T(8,128)}, u32[]{:S(2)}) copy-start(f32[2,12,576]{2,1,0:T(8,128)} %get-tuple-element.369) | copy-start | bytes 165892 | tf_op jit(solution)/shard_map/while
  99.8 11.1 %copy-start.14 = (f32[12,576]{1,0:T(8,128)S(1)}, f32[12,576]{1,0:T(8,128)}, u32[]{:S(2)}) copy-start(f32[12,576]{1,0:T(8,128)} %get-tuple-element.348) | copy-start | bytes 82948 | tf_op jit(solution)/shard_map/while
  99.8 11.1 %copy-start.15 = (f32[12,576]{1,0:T(8,128)S(1)}, f32[12,576]{1,0:T(8,128)}, u32[]{:S(2)}) copy-start(f32[12,576]{1,0:T(8,128)} %fusion.143) | copy-start | bytes 82948 | tf_op jit(solution)/shard_map/while
  99.8 11.1 %copy-start.23 = (f32[2,12,576]{2,1,0:T(8,128)S(1)}, f32[2,12,576]{2,1,0:T(8,128)}, u32[]{:S(2)}) copy-start(f32[2,12,576]{2,1,0:T(8,128)} %get-tuple-element.369) | copy-start | bytes 165892 | tf_op jit(solution)/shard_map/while
  126.9 10.1 %copy-start.54 = (bf16[1,768]{1,0:T(2,128)(2,1)S(1)}, bf16[1,768]{1,0:T(2,128)(2,1)}, u32[]{:S(2)}) copy-start(bf16[1,768]{1,0:T(2,128)(2,1)} %param.39) | copy-start | bytes 4612
  127.0 28.7 %all-to-all-start = ((bf16[8,144,768]{2,1,0:T(8,128)(2,1)}), bf16[8,144,768]{2,1,0:T(8,128)(2,1)}, u32[]{:S(2)}, u32[]{:S(2)}) async-start(bf16[8,144,768]{2,1,0:T(8,128)(2,1)} %bitcast.175), calls=%async_computation | async-start | bytes 3538944 | tf_op jit(solution)/shard_map/all_to_all | solution.py:185
  133.1 22.6 %copy-start.50 = (f32[1,3072]{1,0:T(1,128)S(1)}, f32[1,3072]{1,0:T(1,128)}, u32[]{:S(2)}) copy-start(f32[1,3072]{1,0:T(1,128)} %add.177) | copy-start | bytes 36868
  155.7 40.7 %copy-start.51 = (f32[768]{0:T(1024)S(1)}, f32[768]{0:T(1024)}, u32[]{:S(2)}) copy-start(f32[768]{0:T(1024)} %convert_reduce_fusion.2) | copy-start | bytes 9220
  155.7 40.7 %copy-start.55 = (bf16[1,3072,768]{2,1,0:T(8,128)(2,1)S(1)}, bf16[1,3072,768]{2,1,0:T(8,128)(2,1)}, u32[]{:S(2)}) copy-start(bf16[1,3072,768]{2,1,0:T(8,128)(2,1)} %param.38) | copy-start | bytes 14155780
  203.2 27.6 %all-to-all-start.1 = ((bf16[8,144,768]{2,1,0:T(8,128)(2,1)}), bf16[8,144,768]{2,1,0:T(8,128)(2,1)}, u32[]{:S(2)}, u32[]{:S(2)}) async-start(bf16[8,144,768]{2,1,0:T(8,128)(2,1)} %bitcast.176), calls=%async_computation.1 | async-start | bytes 3538944 | tf_op jit(solution)/shard_map/all_to_all | solution.py:197
  207.7 135.9 %reduce-scatter.15.cloned.1.call-start = ((), (), s32[]{:S(2)}) async-start(), calls=%async_computation.11 | async-start | bytes 245760
  278.8 67.6 %reduce-scatter.13.cloned.1.call-start = ((), (), s32[]{:S(2)}) async-start(), calls=%async_computation.10 | async-start | bytes 983040
  301.7 291.7 %reduce-scatter.11.cloned.1.call-start = ((), (), s32[]{:S(2)}) async-start(), calls=%async_computation.9 | async-start | bytes 5898240 | tf_op jit(solution)/shard_map/reduce_scatter | solution.py:247
  324.2 27.6 %all-to-all-start.3 = ((bf16[8,144,768]{2,1,0:T(8,128)(2,1)}), bf16[8,144,768]{2,1,0:T(8,128)(2,1)}, u32[]{:S(2)}, u32[]{:S(2)}) async-start(bf16[8,144,768]{2,1,0:T(8,128)(2,1)} %bitcast.174), calls=%async_computation.3 | async-start | bytes 3538944 | tf_op jit(solution)/shard_map/all_to_all | solution.py:233
  328.7 267.6 %reduce-scatter.9.cloned.1.call-start = ((), (), s32[]{:S(2)}) async-start(), calls=%async_computation.8 | async-start | bytes 5898240 | tf_op jit(solution)/shard_map/reduce_scatter | solution.py:241
  343.5 362.0 %all-reduce.4.cloned.1.call-start = ((), (), s32[]{:S(2)}) async-start(), calls=%async_computation.12 | async-start | bytes 18874368 | tf_op jit(solution)/shard_map/psum | solution.py:302
  351.8 10.1 %slice-start = ((s8[7077888]{0:T(1024)(128)(4,1)}), s8[4194304]{0:T(1024)(128)(4,1)S(1)}, s32[]{:S(2)}) async-start(s8[7077888]{0:T(1024)(128)(4,1)} %bitcast.164), calls=%async_computation.13 | async-start | bytes 8388608
  351.9 10.0 %slice-start.1 = ((s8[7077888]{0:T(1024)(128)(4,1)}), s8[2883584]{0:T(1024)(128)(4,1)S(1)}, s32[]{:S(2)}) async-start(s8[7077888]{0:T(1024)(128)(4,1)} %bitcast.164), calls=%async_computation.14 | async-start | bytes 5767168
  372.1 131.4 %copy-start.32 = (f32[1152]{0:T(1024)S(1)}, f32[1152]{0:T(1024)}, u32[]{:S(2)}) copy-start(f32[1152]{0:T(1024)} %copy-done.31) | copy-start | bytes 13828
  372.1 131.4 %copy-start.39 = (f32[1152]{0:T(1024)S(1)}, f32[1152]{0:T(1024)}, u32[]{:S(2)}) copy-start(f32[1152]{0:T(1024)} %copy-done.38) | copy-start | bytes 13828
  (53 other events, 218.7 us)
Sparse Core Ops, SparseCore 0:
  278.9 19.2 reduce-scatter.14
  301.9 23.1 reduce-scatter.12
  327.4 84.5 reduce-scatter.10
  414.1 85.8 reduce-scatter.8
Sparse Core Ops, SparseCore 1:
  514.7 190.8 all-reduce.3
where the time goes:
time: 728 us; the launch traced here: 721 us
  matrix products  275 us (38%)
  waiting for transfers between devices  141 us (19%)
  local copies, waits for them, and re-layouts  108 us (15%)
  other arithmetic  96.2 us (13%)
  blocking collectives  67.9 us (9%)
  between operations  16.1 us (2%)
  starting transfers between devices  14.7 us (2%)
    psum x1, waiting for transfers between devices, on_device(): lax.psum((local_qkv, local_q_bias, local_v_bias, local_proj, local_proj_b...  106 us
    unnamed x123, local copies, waits for them, and re-layouts  48.4 us
    dot_general x6, matrix products, contract_first(): lax.dot_general(left, right, (((0,), (0,)), ((), ())), preferred_element_...  44.9 us
    dot_general x4, matrix products, contract_last(): lax.dot_general(left, right, (((1,), (1,)), ((), ())), preferred_element_...  43.2 us
    psum x1, blocking collectives, on_device(): lax.psum((local_qkv, local_q_bias, local_v_bias, local_proj, local_proj_b...  41.6 us
    dot_general x1, matrix products, on_device(): jnp.dot(arrived, weight_in, preferred_element_type=jnp.float32) + bias_in  40.7 us
    dot_general x4, matrix products, image_scores(): jnp.einsum('qhd,khd->hqk', by_heads(queries), by_heads(key_rows), preferr...  31.1 us
    all_to_all x1, blocking collectives, on_device(): lax.all_to_all(grad_returned, 'exp', split_axis=0, concat_axis=0, tiled=T...  26.2 us
  transfers between devices with their start and end apart: 8, of which 4 were waited for; matrix products, arithmetic and copies ran while one was open for 39% of the time, Pallas kernels for 0%

commit v1 on v0

--- a/solution.py
+++ b/solution.py
@@ -8,6 +8,11 @@
 SEQ = 576
 EPSILON = 1e-06
 HIGHEST = lax.Precision.HIGHEST
+
+
+def by_each_axis(x, one, other):
+    half = lax.psum(x, one)
+    return lax.psum(half, other)
 
 
 def norm_forward(field, norm_gain, norm_shift):
@@ -299,7 +304,7 @@
         grad_gain_two,
         grad_shift_two,
         grad_w_router,
-    ) = lax.psum(
+    ) = by_each_axis(
         (
             local_qkv,
             local_q_bias,
@@ -312,7 +317,8 @@
             local_shift_two,
             local_router,
         ),
-        ("rep", "exp"),
+        "exp",
+        "rep",
     )
     return (
         mixed,

time: 728 us -> 1070 us (1.47)
  waiting for transfers between devices: 141 us -> 481 us
    psum x1 -> x2, waiting for transfers between devices: 106 us -> 426 us  [the longest x1 315 us: by_each_axis(): return lax.psum(half, other)]
    all_to_all x1, waiting for transfers between devices: 2.62 us -> 21.8 us  [on_device(): lax.all_to_all(grad_arrived, 'exp', split_axis=0, concat_axis=0, tiled=True)]
    psum x1 -> x2, blocking collectives: 41.6 us -> 48.1 us  [the longest x1 26.2 us: by_each_axis(): half = lax.psum(x, one)]
    unnamed x123 -> x131, local copies, waits for them, and re-layouts: 48.4 us -> 47.4 us
  transfers between devices with their start and end apart: 8 -> 9, of which waited for: 4 -> 5; matrix products, arithmetic and copies ran while one was open for 39% -> 8% of each run, Pallas kernels for 0% -> 0%
where the time goes in v1:
time: 1070 us; the launch traced here: 1060 us
  waiting for transfers between devices  481 us (45%)
  matrix products  274 us (26%)
  local copies, waits for them, and re-layouts  107 us (10%)
  other arithmetic  92.3 us (9%)
  blocking collectives  74.6 us (7%)
  between operations  16.9 us (2%)
  starting transfers between devices  15.4 us (1%)
    psum x1, waiting for transfers between devices, by_each_axis(): return lax.psum(half, other)  315 us
    psum x1, waiting for transfers between devices, by_each_axis(): half = lax.psum(x, one)  112 us
    unnamed x131, local copies, waits for them, and re-layouts  47.4 us
    dot_general x6, matrix products, contract_first(): lax.dot_general(left, right, (((0,), (0,)), ((), ())), preferred_element_...  44.8 us
    dot_general x4, matrix products, contract_last(): lax.dot_general(left, right, (((1,), (1,)), ((), ())), preferred_element_...  42.6 us
    dot_general x1, matrix products, on_device(): jnp.dot(arrived, weight_in, preferred_element_type=jnp.float32) + bias_in  40.7 us
    dot_general x4, matrix products, image_scores(): jnp.einsum('qhd,khd->hqk', by_heads(queries), by_heads(key_rows), preferr...  31 us
    all_to_all x1, blocking collectives, on_device(): lax.all_to_all(grad_returned, 'exp', split_axis=0, concat_axis=0, tiled=T...  26.5 us
  transfers between devices with their start and end apart: 9, of which 5 were waited for; matrix products, arithmetic and copies ran while one was open for 8% of the time, Pallas kernels for 0%

profile of v1, /device:TPU:0, one launch (start us, length us, event | category | flops | bytes accessed | tf_op | source)
XLA Modules:
  0.0 1062.2 jit_solution(18850700597638353)
XLA Ops:
  40.2 75.8 %while.22 = (s32[]{:T(128)}, bf16[2,576,768]{2,1,0:T(8,128)(2,1)}, f32[2,12,576]{2,1,0:T(8,128)}, bf16[2,576,768]{1,2,0:T(8,128)(2,1)}, bf16[2,576,768]{1,2,0:T(...) while((s32[]{:T(128)}, bf16[2,576,768]{2,1,0:T(8,128)(2,1)}, f32[2,12,576]{2,1,0:T(8,128)}, ...), condition=%wide.region_5.6_spmd, body=%wide.region_2.5_spmd.sunk | while | flops 1055040768 | bytes 61086932 | solution.py:164
  62.0 11.1 %fusion.144 = bf16[12,64,576]{2,1,0:T(8,128)(2,1)} fusion(bf16[576,12,64]{0,2,1:T(8,128)(2,1)} %bitcast.167, f32[12,576,576]{1,2,0:T(8,128)} %get-tuple-element.357, f32[12,576]{1,0:T(8,128)} %fusion.143, f32[12,576]{1,0:T(8,128)} %get-tuple-element.358), kind=kOutput, calls=%fused_computation.4.clone.1 | convolution fusion | flops 525533184 | bytes 17750016 | tf_op jit(solution)/shard_map/while/body/eval_jaxpr/hqk,khd->qhd/dot_general | solution.py:77
  99.7 11.1 %fusion.144 = bf16[12,64,576]{2,1,0:T(8,128)(2,1)} fusion(bf16[576,12,64]{0,2,1:T(8,128)(2,1)} %bitcast.167, f32[12,576,576]{1,2,0:T(8,128)} %get-tuple-element.357, f32[12,576]{1,0:T(8,128)} %fusion.143, f32[12,576]{1,0:T(8,128)} %get-tuple-element.358), kind=kOutput, calls=%fused_computation.4.clone.1 | convolution fusion | flops 525533184 | bytes 17750016 | tf_op jit(solution)/shard_map/while/body/eval_jaxpr/hqk,khd->qhd/dot_general | solution.py:77
  141.1 14.5 %all-to-all-done = bf16[8,144,768]{2,1,0:T(8,128)(2,1)} async-done(((bf16[8,144,768]{2,1,0:T(8,128)(2,1)}), bf16[8,144,768]{2,1,0:T(8,128)(2,1)}, u32[]{:S(2)}, u32[]{:S(2)}) %all-to-all-start) | async-done | bytes 1769504 | tf_op jit(solution)/shard_map/all_to_all | solution.py:190
  155.7 40.7 %multiply_convert_fusion.3 = (bf16[1152,3072]{1,0:T(8,128)(2,1)S(1)}, f32[1152,3072]{1,0:T(8,128)}, f32[1152,3072]{1,0:T(8,128)}) fusion(f32[3072]{0:T(1024)S(1)} %bitcast.180, bf16[1152,768]{1,0:T(8,128)(2,1)} %bitcast.20, bf16[1,768,3072]{2,1,0:T(8,128)(2,1)} %param.36), kind=kOutput, calls=%fused_computation.32 | convolution fusion | flops 5669388288 | bytes 41889792 | tf_op jit(solution)/shard_map/dot_general | solution.py:197
  213.0 18.0 %all-to-all-done.1 = bf16[8,144,768]{2,1,0:T(8,128)(2,1)} async-done(((bf16[8,144,768]{2,1,0:T(8,128)(2,1)}), bf16[8,144,768]{2,1,0:T(8,128)(2,1)}, u32[]{:S(2)}, u32[]{:S(2)}) %all-to-all-start.1) | async-done | bytes 1769504 | tf_op jit(solution)/shard_map/all_to_all | solution.py:202
  248.7 26.5 %all_to_all.20 = bf16[8,144,768]{2,1,0:T(8,128)(2,1)} all-to-all(bf16[8,144,768]{2,1,0:T(8,128)(2,1)S(1)} %bitcast.177), channel_id=1, replica_groups=mesh['rep'=4,'exp'=8] {'exp'}, dimensions={0} | all-to-all | bytes 3538944 | tf_op jit(solution)/shard_map/all_to_all | solution.py:229
  275.2 20.3 %fusion.86 = (bf16[3072]{0:T(1024)(128)(2,1)}, bf16[1152,3072]{1,0:T(8,128)(2,1)}) fusion(f32[1152,3072]{1,0:T(8,128)} %get-tuple-element.247, f32[1152,3072]{1,0:T(8,128)} %get-tuple-element.264, bf16[1152,768]{1,0:T(8,128)(2,1)} %bitcast.169, bf16[1,3072,768]{2,1,0:T(8,128)(2,1)} %param.38), kind=kOutput, calls=%fused_computation.154 | convolution fusion | flops 5488899072 | bytes 41883648 | tf_op jit(solution)/shard_map/dot_general | solution.py:43
  295.5 10.3 fusion.55
  311.4 21.8 %all-to-all-done.3 = bf16[8,144,768]{2,1,0:T(8,128)(2,1)} async-done(((bf16[8,144,768]{2,1,0:T(8,128)(2,1)}), bf16[8,144,768]{2,1,0:T(8,128)(2,1)}, u32[]{:S(2)}, u32[]{:S(2)}) %all-to-all-start.3) | async-done | bytes 1769504 | tf_op jit(solution)/shard_map/all_to_all | solution.py:238
  353.5 129.7 %while.23 = (s32[]{:T(128)}, bf16[2,576,2304]{2,1,0:T(8,128)(2,1)}, bf16[2,576,768]{1,2,0:T(8,128)(2,1)}, bf16[2,576,768]{1,2,0:T(8,128)(2,1)}, f32[2,12,576]{2,...) while((s32[]{:T(128)}, bf16[2,576,2304]{2,1,0:T(8,128)(2,1)}, ...), condition=%wide.region_19.20_spmd, body=%wide.region_17.19_spmd.sunk | while | flops 2605982976 | bytes 160441552 | solution.py:276
  369.9 10.1 fusion.156
  380.0 11.6 %multiply_reduce_fusion.11 = (f32[12,576]{1,0:T(8,128)S(1)}, f32[12,576,576]{1,2,0:T(8,128)}) fusion(f32[12,576,576]{1,2,0:T(8,128)} %fusion.155, f32[12,576]{1,0:T(8,128)S(1)} %copy-done.11, bf16[576,12,64]{0,2,1:T(8,128)(2,1)S(1)} %bitcast.155, bf16[576,12,64]{0,2,1:T(8,128)(2,1)S(1)} %bitcast.160), kind=kOutput, calls=%fused_computation.12.clone.1 | convolution fusion | flops 525526272 | bytes 33675264 | tf_op jit(solution)/shard_map/while/body/eval_jaxpr/qhd,khd->hqk/dot_general | solution.py:89
  391.7 12.4 %multiply_convert_fusion.7 = bf16[12,576,576]{1,2,0:T(8,128)(2,1)S(1)} fusion(f32[12,576,576]{1,2,0:T(8,128)} %get-tuple-element.368, f32[12,576,576]{1,2,0:T(8,128)} %fusion.155, f32[12,576]{1,0:T(8,128)S(1)} %get-tuple-element.369, f32[12,576]{1,0:T(8,128)S(1)} %copy-done.11), kind=kLoop, calls=%fused_computation.11.clone.1 | loop fusion | flops 19906560 | bytes 39868416 | tf_op jit(solution)/shard_map/while/body/eval_jaxpr/convert_element_type | solution.py:97
  434.5 10.1 fusion.156
  444.7 11.6 %multiply_reduce_fusion.11 = (f32[12,576]{1,0:T(8,128)S(1)}, f32[12,576,576]{1,2,0:T(8,128)}) fusion(f32[12,576,576]{1,2,0:T(8,128)} %fusion.155, f32[12,576]{1,0:T(8,128)S(1)} %copy-done.11, bf16[576,12,64]{0,2,1:T(8,128)(2,1)S(1)} %bitcast.155, bf16[576,12,64]{0,2,1:T(8,128)(2,1)S(1)} %bitcast.160), kind=kOutput, calls=%fused_computation.12.clone.1 | convolution fusion | flops 525526272 | bytes 33675264 | tf_op jit(solution)/shard_map/while/body/eval_jaxpr/qhd,khd->hqk/dot_general | solution.py:89
  456.3 12.4 %multiply_convert_fusion.7 = bf16[12,576,576]{1,2,0:T(8,128)(2,1)S(1)} fusion(f32[12,576,576]{1,2,0:T(8,128)} %get-tuple-element.368, f32[12,576,576]{1,2,0:T(8,128)} %fusion.155, f32[12,576]{1,0:T(8,128)S(1)} %get-tuple-element.369, f32[12,576]{1,0:T(8,128)S(1)} %copy-done.11), kind=kLoop, calls=%fused_computation.11.clone.1 | loop fusion | flops 19906560 | bytes 39868416 | tf_op jit(solution)/shard_map/while/body/eval_jaxpr/convert_element_type | solution.py:97
  483.2 11.1 %fusion.78 = f32[768,2304]{1,0:T(8,128)} fusion(bf16[1152,2304]{1,0:T(8,128)(2,1)} %bitcast.172, bf16[1152,768]{0,1:T(8,128)(2,1)} %copy.98, f32[768]{0:T(1024)} %param.32, f32[768]{0:T(1024)} %param.31, f32[1152]{0:T(1024)S(1)} %copy-done.42, f32[1152]{0:T(1024)S(1)} %copy-done.32), kind=kOutput, calls=%fused_computation.149 | convolution fusion | flops 4082171904 | bytes 14171136 | tf_op jit(solution)/shard_map/dot_general | solution.py:49
  499.2 11.1 %fusion.28 = bf16[1,3072,768]{2,1,0:T(8,128)(2,1)} fusion(bf16[1152,3072]{1,0:T(8,128)(2,1)} %copy-done.63, bf16[1152,768]{1,0:T(8,128)(2,1)} %bitcast.170), kind=kOutput, calls=%fused_computation.71 | convolution fusion | flops 5438177280 | bytes 13565952 | tf_op jit(solution)/shard_map/dot_general | solution.py:49
  510.4 10.7 %fusion.27 = bf16[1,768,3072]{2,1,0:T(8,128)(2,1)} fusion(bf16[1152,768]{1,0:T(8,128)(2,1)} %bitcast.20, bf16[1152,3072]{1,0:T(8,128)(2,1)} %get-tuple-element.271), kind=kOutput, calls=%fused_computation.70 | convolution fusion | flops 5438177280 | bytes 13565952 | tf_op jit(solution)/shard_map/dot_general | solution.py:49
  521.1 111.5 %all-reduce.7.cloned.1.call-done = (f32[768,2304]{1,0:T(8,128)}, f32[768,768]{1,0:T(8,128)}) async-done(((f32[768,2304]{1,0:T(8,128)}, f32[768,768]{1,0:T(8,128)}), (f32[768,2304]{1,0:T(8,128)}, f32[768,768]{1,0:T(8,128)})) %all-reduce.7.cloned.1.call-update) | async-done | bytes 9437200 | tf_op jit(solution)/shard_map/psum | solution.py:14
  677.2 26.2 %all-reduce = (f32[768]{0:T(1024)}, f32[768]{0:T(1024)}, f32[768]{0:T(1024)}, f32[768]{0:T(1024)}, f32[768]{0:T(1024)}, /*index=5*/f32[768]{0:T(1024)}, f32[768]{0:T(1024)}, f32[768,8]{0,1:T(8,128)}) all-reduce(f32[768]{0:T(1024)S(1)} %get-tuple-element.182, ...), channel_id=1, replica_groups=mesh['rep'=4,'exp'=8] {'exp'}, use_global_device_ids=true, to_apply=%region_25.26 | all-reduce | flops 11520 | bytes 92160 | tf_op jit(solution)/shard_map/psum | solution.py:14
  703.5 21.9 %all-reduce.2 = (f32[768]{0:T(1024)}, f32[768]{0:T(1024)}, f32[768]{0:T(1024)}, f32[768]{0:T(1024)}, f32[768]{0:T(1024)}, /*index=5*/f32[768]{0:T(1024)}, f32[768]{0:T(1024)}, f32[768,8]{0,1:T(8,128)}) all-reduce(f32[768]{0:T(1024)} %get-tuple-element.224, f32[768]{0:T(1024)} %get-tuple-element.225, ...), channel_id=1, replica_groups=mesh['rep'=4,'exp'=8] {'rep'}, use_global_device_ids=true, to_apply=%region_26.27 | all-reduce | flops 11520 | bytes 92160 | tf_op jit(solution)/shard_map/psum | solution.py:15
  731.3 314.8 %all-reduce.9.cloned.1.call-done = (f32[768,2304]{1,0:T(8,128)}, f32[768,768]{1,0:T(8,128)}) async-done(((f32[768,2304]{1,0:T(8,128)}, f32[768,768]{1,0:T(8,128)}), (f32[768,2304]{1,0:T(8,128)}, f32[768,768]{1,0:T(8,128)})) %all-reduce.9.cloned.1.call-update) | async-done | bytes 9437200 | tf_op jit(solution)/shard_map/psum | solution.py:15
  (275 shorter events, 294.5 us)
Async XLA Ops:
  8.0 12.2 %copy-start = (bf16[768,2304]{1,0:T(8,128)(2,1)S(1)}, bf16[768,2304]{1,0:T(8,128)(2,1)}, u32[]{:S(2)}) copy-start(bf16[768,2304]{1,0:T(8,128)(2,1)} %param.26) | copy-start | bytes 10616836
  40.2 75.8 %copy-start.56 = (f32[768]{0:T(1024)S(1)}, f32[768]{0:T(1024)}, u32[]{:S(2)}) copy-start(f32[768]{0:T(1024)} %convert_element_type.153) | copy-start | bytes 9220
  62.0 11.1 %copy-start.14 = (f32[12,576]{1,0:T(8,128)S(1)}, f32[12,576]{1,0:T(8,128)}, u32[]{:S(2)}) copy-start(f32[12,576]{1,0:T(8,128)} %get-tuple-element.358) | copy-start | bytes 82948 | tf_op jit(solution)/shard_map/while
  62.0 11.1 %copy-start.15 = (f32[12,576]{1,0:T(8,128)S(1)}, f32[12,576]{1,0:T(8,128)}, u32[]{:S(2)}) copy-start(f32[12,576]{1,0:T(8,128)} %fusion.143) | copy-start | bytes 82948 | tf_op jit(solution)/shard_map/while
  62.0 11.1 %copy-start.23 = (f32[2,12,576]{2,1,0:T(8,128)S(1)}, f32[2,12,576]{2,1,0:T(8,128)}, u32[]{:S(2)}) copy-start(f32[2,12,576]{2,1,0:T(8,128)} %get-tuple-element.379) | copy-start | bytes 165892 | tf_op jit(solution)/shard_map/while
  99.7 11.1 %copy-start.14 = (f32[12,576]{1,0:T(8,128)S(1)}, f32[12,576]{1,0:T(8,128)}, u32[]{:S(2)}) copy-start(f32[12,576]{1,0:T(8,128)} %get-tuple-element.358) | copy-start | bytes 82948 | tf_op jit(solution)/shard_map/while
  99.7 11.1 %copy-start.15 = (f32[12,576]{1,0:T(8,128)S(1)}, f32[12,576]{1,0:T(8,128)}, u32[]{:S(2)}) copy-start(f32[12,576]{1,0:T(8,128)} %fusion.143) | copy-start | bytes 82948 | tf_op jit(solution)/shard_map/while
  99.7 11.1 %copy-start.23 = (f32[2,12,576]{2,1,0:T(8,128)S(1)}, f32[2,12,576]{2,1,0:T(8,128)}, u32[]{:S(2)}) copy-start(f32[2,12,576]{2,1,0:T(8,128)} %get-tuple-element.379) | copy-start | bytes 165892 | tf_op jit(solution)/shard_map/while
  126.6 10.4 copy-start.58
  126.6 29.0 %all-to-all-start = ((bf16[8,144,768]{2,1,0:T(8,128)(2,1)}), bf16[8,144,768]{2,1,0:T(8,128)(2,1)}, u32[]{:S(2)}, u32[]{:S(2)}) async-start(bf16[8,144,768]{2,1,0:T(8,128)(2,1)} %bitcast.174), calls=%async_computation | async-start | bytes 3538944 | tf_op jit(solution)/shard_map/all_to_all | solution.py:190
  133.1 22.6 %copy-start.54 = (f32[1,3072]{1,0:T(1,128)S(1)}, f32[1,3072]{1,0:T(1,128)}, u32[]{:S(2)}) copy-start(f32[1,3072]{1,0:T(1,128)} %add.197) | copy-start | bytes 36868
  155.7 40.7 %copy-start.55 = (f32[768]{0:T(1024)S(1)}, f32[768]{0:T(1024)}, u32[]{:S(2)}) copy-start(f32[768]{0:T(1024)} %convert_reduce_fusion.2) | copy-start | bytes 9220
  155.7 40.7 %copy-start.59 = (bf16[1,3072,768]{2,1,0:T(8,128)(2,1)S(1)}, bf16[1,3072,768]{2,1,0:T(8,128)(2,1)}, u32[]{:S(2)}) copy-start(bf16[1,3072,768]{2,1,0:T(8,128)(2,1)} %param.38) | copy-start | bytes 14155780
  203.2 27.8 %all-to-all-start.1 = ((bf16[8,144,768]{2,1,0:T(8,128)(2,1)}), bf16[8,144,768]{2,1,0:T(8,128)(2,1)}, u32[]{:S(2)}, u32[]{:S(2)}) async-start(bf16[8,144,768]{2,1,0:T(8,128)(2,1)} %bitcast.176), calls=%async_computation.1 | async-start | bytes 3538944 | tf_op jit(solution)/shard_map/all_to_all | solution.py:202
  305.8 27.5 %all-to-all-start.3 = ((bf16[8,144,768]{2,1,0:T(8,128)(2,1)}), bf16[8,144,768]{2,1,0:T(8,128)(2,1)}, u32[]{:S(2)}, u32[]{:S(2)}) async-start(bf16[8,144,768]{2,1,0:T(8,128)(2,1)} %bitcast.175), calls=%async_computation.3 | async-start | bytes 3538944 | tf_op jit(solution)/shard_map/all_to_all | solution.py:238
  310.1 322.5 %all-reduce.7.cloned.1.call-start = ((), (), s32[]{:S(2)}) async-start(), calls=%async_computation.12 | async-start | bytes 18874368 | tf_op jit(solution)/shard_map/psum | solution.py:14
  311.4 26.8 %copy-start.34 = (f32[1152]{0:T(1024)}, f32[1152]{0:T(1024)S(1)}, u32[]{:S(2)}) copy-start(f32[1152]{0:T(1024)S(1)} %multiply_reduce_fusion.7) | copy-start | bytes 13828
  353.5 129.7 %copy-start.32 = (f32[1152]{0:T(1024)S(1)}, f32[1152]{0:T(1024)}, u32[]{:S(2)}) copy-start(f32[1152]{0:T(1024)} %copy-done.31) | copy-start | bytes 13828
  353.5 129.7 %copy-start.42 = (f32[1152]{0:T(1024)S(1)}, f32[1152]{0:T(1024)}, u32[]{:S(2)}) copy-start(f32[1152]{0:T(1024)} %copy-done.41) | copy-start | bytes 13828
  494.3 142.6 %reduce-scatter.15.cloned.1.call-start = ((), (), s32[]{:S(2)}) async-start(), calls=%async_computation.11 | async-start | bytes 245760
  497.1 141.4 %reduce-scatter.13.cloned.1.call-start = ((), (), s32[]{:S(2)}) async-start(), calls=%async_computation.10 | async-start | bytes 983040
  499.2 226.2 %reduce-scatter.11.cloned.1.call-start = ((), (), s32[]{:S(2)}) async-start(), calls=%async_computation.9 | async-start | bytes 5898240 | tf_op jit(solution)/shard_map/reduce_scatter | solution.py:252
  510.3 218.1 %reduce-scatter.9.cloned.1.call-start = ((), (), s32[]{:S(2)}) async-start(), calls=%async_computation.8 | async-start | bytes 5898240 | tf_op jit(solution)/shard_map/reduce_scatter | solution.py:246
  521.1 525.1 %all-reduce.9.cloned.1.call-start = ((), (), s32[]{:S(2)}) async-start(), calls=%async_computation.13 | async-start | bytes 18874368 | tf_op jit(solution)/shard_map/psum | solution.py:15
  (58 other events, 252.1 us)
Sparse Core Ops, SparseCore 0:
  494.5 138.1 all-reduce.6
Sparse Core Ops, SparseCore 1:
  497.6 19.3 reduce-scatter.14
  519.8 21.2 reduce-scatter.12
  543.3 84.6 reduce-scatter.10
  630.4 86.9 reduce-scatter.8
  719.9 326.2 all-reduce.8
